TPU v7x, 32 devices: a whole 2x2x4 slice. The times are simulated.
32 devices in a mesh: parts: 2 (over y), occ: 8 (over z, core), aux: 2 (over x).
Axes of the slice: x: 2, y: 2, z: 4, core: 2. Of those that a mesh axis runs over, the one named last changes fastest.
Arguments:
- raw_ints: bfloat16 [32, 256, 512], P('parts', 'aux', 'occ'), parts along dimension 0, may hold values from -0.375 to 0.375
- kept: int32 [16, 4, 4], P('parts'), parts along dimension 0, may hold values from 0 to 128
- eps_occ: bfloat16 [32], P(('parts', 'occ')), parts along dimension 0, may hold values from -1.1953125 to -0.3984375
- eps_vir: bfloat16 [512], P('parts'), parts along dimension 0, may hold values from 0.29882812 to 3
- metric_factor: bfloat16 [512, 512], replicated, may hold values from -0.25 to 0.25
Outputs:
- pair_energy: float32 [32, 16], P(('parts', 'occ'), 'aux'), parts along dimension 0
There are 2 independent parts, one for each index of `parts`. A program takes and returns all parts, laid end to end along the dimension named above; an argument that names none is the same for every part. Nothing has to cross between parts.
All inputs are finite; a program needn't handle non-finite values.
Results may differ from a plain program's by a relative error of at most 0.0003.
Values may be sent and summed in bfloat16 or wider, within the bound.
A program may use at most 64 MiB of HBM per device.

v0:
```python
import jax
import jax.numpy as jnp
from jax import lax
from jax.sharding import PartitionSpec as P

VB = 64
PB = 128


def pair_terms(
    left_slice, right_all, left_cols, right_slice, own_levels, part_levels, vir_rows, vir_cols
):
    direct = jnp.einsum("iap,jbp->iajb", left_slice, right_all, preferred_element_type=jnp.float32)
    swapped = jnp.einsum(
        "ibp,jap->iajb", left_cols, right_slice, preferred_element_type=jnp.float32
    )
    own_f = own_levels.astype(jnp.float32)
    part_f = part_levels.astype(jnp.float32)
    rows_f = vir_rows.astype(jnp.float32)
    cols_f = vir_cols.astype(jnp.float32)
    denom = (
        rows_f[None, :, None, None]
        + cols_f[None, None, None, :]
        - own_f[:, None, None, None]
        - part_f[None, None, :, None]
    )
    return -jnp.sum(direct * (2.0 * direct - swapped) / denom, axis=(1, 3))


def body(raw_ints, kept, eps_occ, eps_vir, metric_factor):
    total_occ = raw_ints.shape[0]
    slice_vir = raw_ints.shape[1]
    slice_aux = raw_ints.shape[2]
    naux_all = metric_factor.shape[0]
    own_occ = eps_occ.shape[0]
    block_count = kept.shape[2]
    occ_index = lax.axis_index("occ")
    aux_index = lax.axis_index("aux")
    repeated = jnp.repeat(jnp.repeat(kept, total_occ // kept.shape[0], axis=0), VB, axis=1)
    kept_vir = lax.dynamic_slice_in_dim(repeated, aux_index * slice_vir, slice_vir, 1)
    aux_start = occ_index * slice_aux
    positions = aux_start + jnp.arange(slice_aux, dtype=jnp.int32)
    block_ids = positions // PB
    onehot = (block_ids[:, None] == jnp.arange(block_count, dtype=jnp.int32)[None, :]).astype(
        jnp.int32
    )
    kept_here = jnp.sum(kept_vir[:, :, None, :] * onehot[None, None, :, :], axis=3)
    offset = positions % PB
    screened = jnp.where(offset[None, None, :] < kept_here, raw_ints, jnp.zeros_like(raw_ints))
    relaid = lax.all_to_all(screened, "occ", split_axis=0, concat_axis=2, tiled=True)
    own_slice = jnp.dot(
        relaid.reshape(own_occ * slice_vir, naux_all),
        metric_factor,
        preferred_element_type=jnp.float32,
    )
    own_slice = own_slice.astype(jnp.bfloat16).reshape(own_occ, slice_vir, naux_all)
    vir_rows = lax.dynamic_slice_in_dim(eps_vir, aux_index * slice_vir, slice_vir)
    empty = jnp.zeros((own_occ, total_occ), jnp.float32)
    own_full = lax.all_gather(own_slice, "aux", axis=1, tiled=True)
    partner_rows = lax.all_gather(own_full, "occ", axis=0, tiled=True)
    partner_levels = lax.all_gather(eps_occ, "occ", axis=0, tiled=True)
    blocks_in = partner_rows.shape[0] // own_occ

    def add_block(block_no, totals):
        part_block = lax.dynamic_slice_in_dim(partner_rows, block_no * own_occ, own_occ, 0)
        part_level = lax.dynamic_slice_in_dim(partner_levels, block_no * own_occ, own_occ, 0)
        part_slice = lax.dynamic_slice_in_dim(part_block, aux_index * slice_vir, slice_vir, 1)
        term = pair_terms(
            own_slice, part_block, own_full, part_slice, eps_occ, part_level, vir_rows, eps_vir
        )
        column = block_no * own_occ
        before = lax.dynamic_slice_in_dim(totals, column, own_occ, 1)
        return lax.dynamic_update_slice_in_dim(totals, before + term, column, 1)

    energies = lax.fori_loop(0, blocks_in, add_block, empty)
    return lax.psum_scatter(energies, "aux", scatter_dimension=1, tiled=True)


def solution(mesh):
    in_specs = (
        P("parts", "aux", "occ"),
        P("parts", None, None),
        P(("parts", "occ")),
        P("parts"),
        P(),
    )
    out_specs = P(("parts", "occ"), "aux")
    return jax.shard_map(body, mesh=mesh, in_specs=in_specs, out_specs=out_specs, check_vma=False)
```

profile of v0, /device:TPU:0, one launch (start us, length us, event | category | flops | bytes accessed | tf_op | source)
XLA Modules:
  0.0 123.0 jit_solution(1432084344117811612)
XLA Ops:
  6.6 0.9 copy.16
  7.5 0.1 broadcast_in_dim.31
  7.6 0.1 reshape.139
  7.8 0.3 multiply_reduce_fusion
  8.1 1.1 compare_select_fusion
  9.2 15.9 %all_to_all.15 = bf16[16,128,64]{1,2,0:T(8,128)(2,1)S(1)} all-to-all(bf16[16,128,64]{1,2,0:T(8,128)(2,1)S(1)} %compare_select_fusion), channel_id=1, replica_groups=mesh['parts'=2,'occ'=8,'aux'=2] {'occ'}, dimensions={0} | all-to-all | bytes 524288 | tf_op jit(solution)/shard_map/all_to_all | solution.py:50
  25.0 0.3 copy.17
  25.3 0.3 convolution_convert_fusion
  25.7 8.5 %all_gather.9 = bf16[2,256,512]{2,1,0:T(8,128)(2,1)} all-gather(bf16[2,128,512]{2,1,0:T(8,128)(2,1)S(1)} %bitcast.58), channel_id=1, replica_groups=mesh['parts'=2,'occ'=8,'aux'=2] {'aux'}, dimensions={1}, use_global_device_ids=true | all-gather | bytes 786432 | tf_op jit(solution)/shard_map/all_gather | solution.py:59
  34.2 0.6 dynamic-slice
  35.4 0.2 dynamic-update-slice
  35.7 14.5 %all-reduce = bf16[16]{0:T(256)(128)(2,1)S(1)} all-reduce(bf16[16]{0:T(256)(128)(2,1)S(1)} %dynamic-update-slice), channel_id=1, replica_groups=mesh['parts'=2,'occ'=8,'aux'=2] {'occ'}, use_global_device_ids=true, to_apply=%add | all-reduce | flops 16 | bytes 64
  50.3 0.6 dynamic-slice.1
  51.6 29.5 %all-gather.2.cloned.1.call-done = bf16[16,256,512]{2,1,0:T(8,128)(2,1)} async-done(((bf16[2,256,512]{2,1,0:T(8,128)(2,1)}), bf16[16,256,512]{2,1,0:T(8,128)(2,1)}) %all-gather.2.cloned.1.call-update) | async-done | bytes 4194320 | tf_op jit(solution)/shard_map/all_gather | solution.py:60
  81.1 29.6 %while.16 = (s32[]{:T(128)}, f32[2,16]{1,0:T(2,128)S(1)}, bf16[16,256,512]{2,1,0:T(8,128)(2,1)}, bf16[2,128,512]{2,1,0:T(8,128)(2,1)S(1)}, s32[]{:T(128)}, /*ind...) while((s32[]{:T(128)}, f32[2,16]{1,0:T(2,128)S(1)}, ...), condition=%wide.region_3.4_spmd, body=%wide.region_1.3_spmd.sunk | while | flops 269320576 | bytes 3412679 | solution.py:75
  81.2 0.1 copy.34
  81.3 0.1 broadcast_add_fusion.2
  81.5 1.4 %convolution_bitcast_fusion.3 = f32[2,128,2,256]{1,3,0,2:T(8,128)S(1)} fusion(bf16[16,256,512]{2,1,0:T(8,128)(2,1)} %get-tuple-element.408, s32[]{:T(128)S(6)} %select_n.63, bf16[2,128,512]{2,1,0:T(8,128)(2,1)S(1)} %get-tuple-element.409), kind=kOutput, calls=%fused_computation.1.clone.1 | convolution fusion | flops 134217728 | bytes 1310724 | tf_op jit(solution)/shard_map/while/body/eval_jaxpr/iap,jbp->iajb/dot_general | solution.py:13
  82.9 1.6 %fusion.25 = f32[2,2]{0,1:T(2,128)S(1)} fusion(f32[2,128,2,256]{1,3,0,2:T(8,128)S(1)} %convolution_bitcast_fusion.3, bf16[2,256,512]{2,1,0:T(8,128)(2,1)} %get-tuple-element.411, f32[2]{0:T(128)S(1)} %dynamic-slice_convert_fusion.2, f32[2,128,256]{1,2,0:T(8,128)S(1)} %broadcast_subtract_fusion.2, bf16[16,256,512]{2,1,0:T(8,128)(2,1)} %get-tuple-element.408, ...), kind=kOutput, calls=%fused_computation.5.clone.1 | convolution fusion | flops 135004160 | bytes 1573404 | tf_op jit(solution)/shard_map/while/body/eval_jaxpr/ibp,jap->iajb/dot_general | solution.py:14
  84.5 0.1 copy.35
  84.8 0.1 copy.34
  84.9 0.1 broadcast_add_fusion.2
  85.1 1.4 %convolution_bitcast_fusion.3 = f32[2,128,2,256]{1,3,0,2:T(8,128)S(1)} fusion(bf16[16,256,512]{2,1,0:T(8,128)(2,1)} %get-tuple-element.408, s32[]{:T(128)S(6)} %select_n.63, bf16[2,128,512]{2,1,0:T(8,128)(2,1)S(1)} %get-tuple-element.409), kind=kOutput, calls=%fused_computation.1.clone.1 | convolution fusion | flops 134217728 | bytes 1310724 | tf_op jit(solution)/shard_map/while/body/eval_jaxpr/iap,jbp->iajb/dot_general | solution.py:13
  86.5 1.6 %fusion.25 = f32[2,2]{0,1:T(2,128)S(1)} fusion(f32[2,128,2,256]{1,3,0,2:T(8,128)S(1)} %convolution_bitcast_fusion.3, bf16[2,256,512]{2,1,0:T(8,128)(2,1)} %get-tuple-element.411, f32[2]{0:T(128)S(1)} %dynamic-slice_convert_fusion.2, f32[2,128,256]{1,2,0:T(8,128)S(1)} %broadcast_subtract_fusion.2, bf16[16,256,512]{2,1,0:T(8,128)(2,1)} %get-tuple-element.408, ...), kind=kOutput, calls=%fused_computation.5.clone.1 | convolution fusion | flops 135004160 | bytes 1573404 | tf_op jit(solution)/shard_map/while/body/eval_jaxpr/ibp,jap->iajb/dot_general | solution.py:14
  88.1 0.1 copy.35
  88.2 0.2 dynamic_update_slice.12
  88.5 0.1 copy.34
  88.6 0.1 broadcast_add_fusion.2
  88.8 1.4 %convolution_bitcast_fusion.3 = f32[2,128,2,256]{1,3,0,2:T(8,128)S(1)} fusion(bf16[16,256,512]{2,1,0:T(8,128)(2,1)} %get-tuple-element.408, s32[]{:T(128)S(6)} %select_n.63, bf16[2,128,512]{2,1,0:T(8,128)(2,1)S(1)} %get-tuple-element.409), kind=kOutput, calls=%fused_computation.1.clone.1 | convolution fusion | flops 134217728 | bytes 1310724 | tf_op jit(solution)/shard_map/while/body/eval_jaxpr/iap,jbp->iajb/dot_general | solution.py:13
  90.2 1.6 %fusion.25 = f32[2,2]{0,1:T(2,128)S(1)} fusion(f32[2,128,2,256]{1,3,0,2:T(8,128)S(1)} %convolution_bitcast_fusion.3, bf16[2,256,512]{2,1,0:T(8,128)(2,1)} %get-tuple-element.411, f32[2]{0:T(128)S(1)} %dynamic-slice_convert_fusion.2, f32[2,128,256]{1,2,0:T(8,128)S(1)} %broadcast_subtract_fusion.2, bf16[16,256,512]{2,1,0:T(8,128)(2,1)} %get-tuple-element.408, ...), kind=kOutput, calls=%fused_computation.5.clone.1 | convolution fusion | flops 135004160 | bytes 1573404 | tf_op jit(solution)/shard_map/while/body/eval_jaxpr/ibp,jap->iajb/dot_general | solution.py:14
  91.8 0.1 copy.35
  91.9 0.2 dynamic_update_slice.12
  92.2 0.1 copy.34
  92.3 0.1 broadcast_add_fusion.2
  92.5 1.4 %convolution_bitcast_fusion.3 = f32[2,128,2,256]{1,3,0,2:T(8,128)S(1)} fusion(bf16[16,256,512]{2,1,0:T(8,128)(2,1)} %get-tuple-element.408, s32[]{:T(128)S(6)} %select_n.63, bf16[2,128,512]{2,1,0:T(8,128)(2,1)S(1)} %get-tuple-element.409), kind=kOutput, calls=%fused_computation.1.clone.1 | convolution fusion | flops 134217728 | bytes 1310724 | tf_op jit(solution)/shard_map/while/body/eval_jaxpr/iap,jbp->iajb/dot_general | solution.py:13
  93.9 1.6 %fusion.25 = f32[2,2]{0,1:T(2,128)S(1)} fusion(f32[2,128,2,256]{1,3,0,2:T(8,128)S(1)} %convolution_bitcast_fusion.3, bf16[2,256,512]{2,1,0:T(8,128)(2,1)} %get-tuple-element.411, f32[2]{0:T(128)S(1)} %dynamic-slice_convert_fusion.2, f32[2,128,256]{1,2,0:T(8,128)S(1)} %broadcast_subtract_fusion.2, bf16[16,256,512]{2,1,0:T(8,128)(2,1)} %get-tuple-element.408, ...), kind=kOutput, calls=%fused_computation.5.clone.1 | convolution fusion | flops 135004160 | bytes 1573404 | tf_op jit(solution)/shard_map/while/body/eval_jaxpr/ibp,jap->iajb/dot_general | solution.py:14
  95.5 0.1 copy.35
  95.6 0.2 dynamic_update_slice.12
  96.0 0.1 copy.34
  96.0 0.1 broadcast_add_fusion.2
  96.2 1.4 %convolution_bitcast_fusion.3 = f32[2,128,2,256]{1,3,0,2:T(8,128)S(1)} fusion(bf16[16,256,512]{2,1,0:T(8,128)(2,1)} %get-tuple-element.408, s32[]{:T(128)S(6)} %select_n.63, bf16[2,128,512]{2,1,0:T(8,128)(2,1)S(1)} %get-tuple-element.409), kind=kOutput, calls=%fused_computation.1.clone.1 | convolution fusion | flops 134217728 | bytes 1310724 | tf_op jit(solution)/shard_map/while/body/eval_jaxpr/iap,jbp->iajb/dot_general | solution.py:13
  97.6 1.6 %fusion.25 = f32[2,2]{0,1:T(2,128)S(1)} fusion(f32[2,128,2,256]{1,3,0,2:T(8,128)S(1)} %convolution_bitcast_fusion.3, bf16[2,256,512]{2,1,0:T(8,128)(2,1)} %get-tuple-element.411, f32[2]{0:T(128)S(1)} %dynamic-slice_convert_fusion.2, f32[2,128,256]{1,2,0:T(8,128)S(1)} %broadcast_subtract_fusion.2, bf16[16,256,512]{2,1,0:T(8,128)(2,1)} %get-tuple-element.408, ...), kind=kOutput, calls=%fused_computation.5.clone.1 | convolution fusion | flops 135004160 | bytes 1573404 | tf_op jit(solution)/shard_map/while/body/eval_jaxpr/ibp,jap->iajb/dot_general | solution.py:14
  99.2 0.1 copy.35
  99.3 0.2 dynamic_update_slice.12
  99.7 0.1 copy.34
  99.8 0.1 broadcast_add_fusion.2
  99.9 1.4 %convolution_bitcast_fusion.3 = f32[2,128,2,256]{1,3,0,2:T(8,128)S(1)} fusion(bf16[16,256,512]{2,1,0:T(8,128)(2,1)} %get-tuple-element.408, s32[]{:T(128)S(6)} %select_n.63, bf16[2,128,512]{2,1,0:T(8,128)(2,1)S(1)} %get-tuple-element.409), kind=kOutput, calls=%fused_computation.1.clone.1 | convolution fusion | flops 134217728 | bytes 1310724 | tf_op jit(solution)/shard_map/while/body/eval_jaxpr/iap,jbp->iajb/dot_general | solution.py:13
  101.3 1.6 %fusion.25 = f32[2,2]{0,1:T(2,128)S(1)} fusion(f32[2,128,2,256]{1,3,0,2:T(8,128)S(1)} %convolution_bitcast_fusion.3, bf16[2,256,512]{2,1,0:T(8,128)(2,1)} %get-tuple-element.411, f32[2]{0:T(128)S(1)} %dynamic-slice_convert_fusion.2, f32[2,128,256]{1,2,0:T(8,128)S(1)} %broadcast_subtract_fusion.2, bf16[16,256,512]{2,1,0:T(8,128)(2,1)} %get-tuple-element.408, ...), kind=kOutput, calls=%fused_computation.5.clone.1 | convolution fusion | flops 135004160 | bytes 1573404 | tf_op jit(solution)/shard_map/while/body/eval_jaxpr/ibp,jap->iajb/dot_general | solution.py:14
  102.9 0.1 copy.35
  103.0 0.2 dynamic_update_slice.12
  103.4 0.1 copy.34
  103.5 0.1 broadcast_add_fusion.2
  103.7 1.4 %convolution_bitcast_fusion.3 = f32[2,128,2,256]{1,3,0,2:T(8,128)S(1)} fusion(bf16[16,256,512]{2,1,0:T(8,128)(2,1)} %get-tuple-element.408, s32[]{:T(128)S(6)} %select_n.63, bf16[2,128,512]{2,1,0:T(8,128)(2,1)S(1)} %get-tuple-element.409), kind=kOutput, calls=%fused_computation.1.clone.1 | convolution fusion | flops 134217728 | bytes 1310724 | tf_op jit(solution)/shard_map/while/body/eval_jaxpr/iap,jbp->iajb/dot_general | solution.py:13
  105.0 1.6 %fusion.25 = f32[2,2]{0,1:T(2,128)S(1)} fusion(f32[2,128,2,256]{1,3,0,2:T(8,128)S(1)} %convolution_bitcast_fusion.3, bf16[2,256,512]{2,1,0:T(8,128)(2,1)} %get-tuple-element.411, f32[2]{0:T(128)S(1)} %dynamic-slice_convert_fusion.2, f32[2,128,256]{1,2,0:T(8,128)S(1)} %broadcast_subtract_fusion.2, bf16[16,256,512]{2,1,0:T(8,128)(2,1)} %get-tuple-element.408, ...), kind=kOutput, calls=%fused_computation.5.clone.1 | convolution fusion | flops 135004160 | bytes 1573404 | tf_op jit(solution)/shard_map/while/body/eval_jaxpr/ibp,jap->iajb/dot_general | solution.py:14
  106.6 0.1 copy.35
  106.7 0.2 dynamic_update_slice.12
  107.1 0.1 copy.34
  107.2 0.1 broadcast_add_fusion.2
  107.4 1.4 %convolution_bitcast_fusion.3 = f32[2,128,2,256]{1,3,0,2:T(8,128)S(1)} fusion(bf16[16,256,512]{2,1,0:T(8,128)(2,1)} %get-tuple-element.408, s32[]{:T(128)S(6)} %select_n.63, bf16[2,128,512]{2,1,0:T(8,128)(2,1)S(1)} %get-tuple-element.409), kind=kOutput, calls=%fused_computation.1.clone.1 | convolution fusion | flops 134217728 | bytes 1310724 | tf_op jit(solution)/shard_map/while/body/eval_jaxpr/iap,jbp->iajb/dot_general | solution.py:13
  108.7 1.6 %fusion.25 = f32[2,2]{0,1:T(2,128)S(1)} fusion(f32[2,128,2,256]{1,3,0,2:T(8,128)S(1)} %convolution_bitcast_fusion.3, bf16[2,256,512]{2,1,0:T(8,128)(2,1)} %get-tuple-element.411, f32[2]{0:T(128)S(1)} %dynamic-slice_convert_fusion.2, f32[2,128,256]{1,2,0:T(8,128)S(1)} %broadcast_subtract_fusion.2, bf16[16,256,512]{2,1,0:T(8,128)(2,1)} %get-tuple-element.408, ...), kind=kOutput, calls=%fused_computation.5.clone.1 | convolution fusion | flops 135004160 | bytes 1573404 | tf_op jit(solution)/shard_map/while/body/eval_jaxpr/ibp,jap->iajb/dot_general | solution.py:14
  110.3 0.1 copy.35
  110.4 0.2 dynamic_update_slice.12
  110.6 4.9 %all-reduce.1 = f32[2,16]{1,0:T(2,128)S(1)} all-reduce(f32[2,16]{1,0:T(2,128)S(1)} %get-tuple-element.292), channel_id=2, replica_groups=mesh['parts'=2,'occ'=8,'aux'=2] {'aux'}, use_global_device_ids=true, to_apply=%region_4.5.clone | all-reduce | flops 32 | bytes 256
  115.5 0.6 constant_dynamic-slice_fusion.1
  (76 shorter events, 2.3 us)
Async XLA Ops:
  6.5 18.8 %copy-start = (bf16[512,512]{1,0:T(8,128)(2,1)S(1)}, bf16[512,512]{1,0:T(8,128)(2,1)}, u32[]{:S(2)}) copy-start(bf16[512,512]{1,0:T(8,128)(2,1)} %param.11) | copy-start | bytes 1572868
  6.5 27.6 %copy-start.4 = (u32[32]{0:T(128)S(1)}, u32[32]{0:T(128)}, u32[]{:S(2)}) copy-start(u32[32]{0:T(128)} %constant.183) | copy-start | bytes 388
  6.5 43.7 %copy-start.3 = (u32[32]{0:T(128)S(1)}, u32[32]{0:T(128)}, u32[]{:S(2)}) copy-start(u32[32]{0:T(128)} %constant.189) | copy-start | bytes 388
  6.5 28.9 %copy-start.2 = (bf16[2]{0:T(256)(128)(2,1)S(1)}, bf16[2]{0:T(256)(128)(2,1)}, u32[]{:S(2)}) copy-start(bf16[2]{0:T(256)(128)(2,1)} %param.9) | copy-start | bytes 16
  6.5 43.7 %copy-start.1 = (bf16[256]{0:T(256)(128)(2,1)S(1)}, bf16[256]{0:T(256)(128)(2,1)}, u32[]{:S(2)}) copy-start(bf16[256]{0:T(256)(128)(2,1)} %param.10) | copy-start | bytes 1540
  6.5 74.5 %all-gather.2.cloned.1.call-start = ((), (), s32[]{:S(2)}) async-start(), calls=%async_computation.1 | async-start | bytes 4718592 | tf_op jit(solution)/shard_map/all_gather | solution.py:60
Sparse Core Ops, SparseCore 0:
  34.3 46.7 all-gather.1
where the time goes:
time: 124 us; the launch traced here: 123 us
  blocking collectives  43.8 us (35%)
  waiting for transfers between devices  29.5 us (24%)
  matrix products  23.9 us (19%)
  between operations  14.8 us (12%)
  local copies, waits for them, and re-layouts  7.17 us (6%)
  other arithmetic  3.58 us (3%)
    all_gather x1, waiting for transfers between devices, body(): partner_rows = lax.all_gather(own_full, 'occ', axis=0, tiled=True)  29.5 us
    unnamed x2, blocking collectives  19.5 us
    all_to_all x1, blocking collectives, body(): lax.all_to_all(screened, 'occ', split_axis=0, concat_axis=2, tiled=True)  15.9 us
    dot_general x8, matrix products, pair_terms(): jnp.einsum('ibp,jap->iajb', left_cols, right_slice, preferred_element_typ...  12.6 us
    dot_general x8, matrix products, pair_terms(): jnp.einsum('iap,jbp->iajb', left_slice, right_all, preferred_element_type...  11 us
    all_gather x1, blocking collectives, body(): own_full = lax.all_gather(own_slice, 'aux', axis=1, tiled=True)  8.46 us
    unnamed x16, local copies, waits for them, and re-layouts  3.01 us
  transfers between devices with their start and end apart: 1, of which 1 were waited for; matrix products, arithmetic and copies ran while one was open for 1% of the time, Pallas kernels for 0%

commit v1 on v0

--- a/solution.py
+++ b/solution.py
@@ -1,10 +1,296 @@
+import functools
+
 import jax
 import jax.numpy as jnp
 from jax import lax
+from jax.experimental import pallas as pl
+from jax.experimental.pallas import tpu as pltpu
 from jax.sharding import PartitionSpec as P
 
 VB = 64
 PB = 128
+MESH = pl.DeviceIdType.MESH
+F32 = jnp.float32
+
+
+def needs(x, z):
+    first = jnp.maximum(z - 1, 0)
+    second = jnp.where(z == 0, 1, jnp.where(z == 3, 3, 2 + x))
+    return first, second
+
+
+def kernel(
+    raw_ref, kept_ref, occ_ref, row_ref, col_ref, metric_ref, out_ref,
+    blocks, mat, fac, base, levels, energy, shares,
+    recv, s_right, s_left, s_aux, s_core, s_lev, r_lev, s_out, r_out,
+):
+    occ = lax.axis_index("occ")
+    x = lax.axis_index("aux")
+    z, c = occ // 2, occ % 2
+    me = occ * 2 + x
+    left_lim = jnp.where(z == 1, 2, 4)
+    left_lim_in = jnp.where(z == 0, 2, 4)
+    own = needs(x, z)
+    other = needs(1 - x, z)
+
+    barrier = pltpu.get_barrier_semaphore()
+    for d in range(1, 16):
+        peer = (me + d) % 16
+        pl.semaphore_signal(
+            barrier, inc=1, device_id={"occ": peer // 2, "aux": peer % 2}, device_id_type=MESH
+        )
+
+    lane = lax.broadcasted_iota(jnp.int32, (2 * VB, 2 * VB), 1) % VB + c * VB
+    row = lax.broadcasted_iota(jnp.int32, (2 * VB, 2 * VB), 0)
+    for k in range(8):
+        both = jnp.concatenate([raw_ref[2 * k], raw_ref[2 * k + 1]], axis=1).astype(F32)
+        limit = jnp.where(row < VB, kept_ref[k, 2 * x, z], kept_ref[k, 2 * x + 1, z])
+        blocks[z, x, c, k // 2, k % 2] = jnp.where(lane < limit, both, 0.0).astype(jnp.bfloat16)
+    levels[occ] = occ_ref[...]
+
+    pl.semaphore_wait(barrier, 15)
+
+    def copy(zs, xs, cs, n, send_sem, to_occ, to_x):
+        return pltpu.make_async_remote_copy(
+            src_ref=blocks.at[zs, xs, cs, n],
+            dst_ref=blocks.at[zs, xs, cs, n],
+            send_sem=send_sem,
+            recv_sem=recv.at[zs, xs, cs, n],
+            device_id={"occ": to_occ, "aux": to_x},
+            device_id_type=MESH,
+        )
+
+    right_id = jnp.minimum(occ + 2, 7)
+    left_id = jnp.maximum(occ - 2, 0)
+    core_id = 2 * z + 1 - c
+
+    def go_right(zs, n):
+        return copy(zs, x, c, n, s_right.at[zs, n], right_id, x)
+
+    def go_left(zs, n):
+        return copy(zs, x, c, n, s_left.at[zs, n], left_id, x)
+
+    def go_aux(zs, m):
+        return copy(zs, x, c, other[m], s_aux.at[zs, m], occ, 1 - x)
+
+    def go_core(zs, xs, m):
+        return copy(zs, xs, c, own[m], s_core.at[zs, xs, m], core_id, x)
+
+    def arrived(zs, xs, cs, n):
+        copy(zs, xs, cs, n, s_right.at[0, 0], core_id, x).wait_recv()
+
+    def spread(zs):
+        for m in range(2):
+            go_aux(zs, m).start()
+        for m in range(2):
+            go_core(zs, x, m).start()
+
+    def take_aux(zs):
+        for m in range(2):
+            arrived(zs, 1 - x, c, own[m])
+            go_core(zs, 1 - x, m).start()
+
+    for n in range(4):
+        @pl.when((z < 3) & (n >= z))
+        def _():
+            go_right(z, n).start()
+
+        @pl.when((z > 0) & (n < left_lim))
+        def _():
+            go_left(z, n).start()
+    spread(z)
+
+    def level_copy(d):
+        to = (occ + d) % 8
+        return pltpu.make_async_remote_copy(
+            src_ref=levels.at[occ], dst_ref=levels.at[occ],
+            send_sem=s_lev.at[d], recv_sem=r_lev.at[d],
+            device_id={"occ": to}, device_id_type=MESH,
+        )
+
+    def level_wait(d):
+        frm = (occ + 8 - d) % 8
+        pltpu.make_async_remote_copy(
+            src_ref=levels.at[frm], dst_ref=levels.at[frm],
+            send_sem=s_lev.at[d], recv_sem=r_lev.at[d],
+            device_id={"occ": (occ + d) % 8}, device_id_type=MESH,
+        ).wait_recv()
+
+    for d in range(1, 8):
+        level_copy(d).start()
+    base[...] = col_ref[...] + row_ref[...]
+    energy[...] = jnp.zeros_like(energy)
+
+    for t in range(1, 4):
+        @pl.when(z >= t)
+        def _():
+            zs = jnp.maximum(z - t, 0)
+            for n in range(4):
+                @pl.when(n >= z - 1)
+                def _():
+                    arrived(zs, x, c, n)
+
+                @pl.when((z < 3) & (n >= z))
+                def _():
+                    go_right(zs, n).start()
+
+        @pl.when(z + t <= 3)
+        def _():
+            zs = jnp.minimum(z + t, 3)
+            for n in range(4):
+                @pl.when(n < left_lim_in)
+                def _():
+                    arrived(zs, x, c, n)
+
+                @pl.when((z > 0) & (n < left_lim))
+                def _():
+                    go_left(zs, n).start()
+
+        @pl.when(z >= t)
+        def _():
+            spread(jnp.maximum(z - t, 0))
+
+        @pl.when(z + t <= 3)
+        def _():
+            spread(jnp.minimum(z + t, 3))
+
+        if t == 1:
+            take_aux(z)
+        else:
+            @pl.when(z >= t - 1)
+            def _():
+                take_aux(jnp.maximum(z - t + 1, 0))
+
+            @pl.when(z + t - 1 <= 3)
+            def _():
+                take_aux(jnp.minimum(z + t - 1, 3))
+
+    @pl.when(z >= 3)
+    def _():
+        take_aux(jnp.maximum(z - 3, 0))
+
+    @pl.when(z + 3 <= 3)
+    def _():
+        take_aux(jnp.minimum(z + 3, 3))
+
+    for zs in range(4):
+        for xs in range(2):
+            for m in range(2):
+                arrived(zs, xs, 1 - c, own[m])
+
+    diag = (x == 0) & ((z == 0) | (z == 3))
+    for kk in range(4):
+        @pl.when((diag & (kk // 2 == c)) | (jnp.logical_not(diag) & ((kk == c) | (kk >= 2))))
+        def _():
+            n = own[kk // 2]
+            for xs in range(2):
+                for zs in range(4):
+                    t0 = blocks[zs, xs, 0, n, kk % 2]
+                    t1 = blocks[zs, xs, 1, n, kk % 2]
+                    mat[pl.ds(xs * 128, 128), pl.ds(zs * 128, 128)] = jnp.concatenate(
+                        [t0[:, :VB], t1[:, :VB]], axis=1)
+                    mat[pl.ds(256 + xs * 128, 128), pl.ds(zs * 128, 128)] = jnp.concatenate(
+                        [t0[:, VB:], t1[:, VB:]], axis=1)
+            prod = jnp.dot(mat[...], metric_ref[...], preferred_element_type=F32)
+            prod = prod.astype(jnp.bfloat16)
+            fac[2 * kk] = prod[:256]
+            fac[2 * kk + 1] = prod[256:]
+
+    for d in range(1, 8):
+        level_wait(d)
+
+    rows8 = lax.broadcasted_iota(jnp.int32, (8, 128), 0)
+    lanes8 = lax.broadcasted_iota(jnp.int32, (8, 128), 1)
+
+    def one_pair(t, carry):
+        li = jnp.where(diag, 4 * c + t % 4, 2 * c + t // 4)
+        lj = jnp.where(diag, 4 * c + (t % 4 + t // 4) % 4, 4 + t % 4)
+        gi = 4 * jnp.where(li < 4, own[0], own[1]) + li % 4
+        gj = 4 * jnp.where(lj < 4, own[0], own[1]) + lj % 4
+        fi, fj = fac[li], fac[lj]
+        dims = (((1,), (1,)), ((), ()))
+        direct = lax.dot_general(fi, fj, dims, preferred_element_type=F32)
+        swapped = lax.dot_general(fj, fi, dims, preferred_element_type=F32)
+        pair_level = levels[gi // 2, pl.ds(gi % 2, 1), :] + levels[gj // 2, pl.ds(gj % 2, 1), :]
+        pair_level = jnp.concatenate([pair_level, pair_level], axis=1)
+        term = direct * (2.0 * direct - swapped) / (base[...] - pair_level)
+        term = -jnp.sum(jnp.sum(term, axis=0, keepdims=True), axis=1, keepdims=True)
+        energy[gi // 2] += jnp.where((rows8 == gi % 2) & (lanes8 == gj), term, 0.0)
+        turned = (rows8 == gj % 2) & (lanes8 == gi) & (gi != gj)
+        energy[gj // 2] += jnp.where(turned, term, 0.0)
+        return carry
+
+    lax.fori_loop(0, jnp.where(diag, 10, 8), one_pair, 0)
+
+    def out_copy(d):
+        to = (me + d) % 16
+        return pltpu.make_async_remote_copy(
+            src_ref=energy.at[to // 2], dst_ref=shares.at[d],
+            send_sem=s_out.at[d], recv_sem=r_out.at[d],
+            device_id={"occ": to // 2, "aux": to % 2}, device_id_type=MESH,
+        )
+
+    for d in range(1, 16):
+        out_copy(d).start()
+
+    for n in range(4):
+        for t in range(4):
+            @pl.when((z >= t) & (z < 3) & (n >= z))
+            def _():
+                go_right(jnp.maximum(z - t, 0), n).wait_send()
+
+            @pl.when((z + t <= 3) & (z > 0) & (n < left_lim))
+            def _():
+                go_left(jnp.minimum(z + t, 3), n).wait_send()
+    for zs in range(4):
+        for m in range(2):
+            go_aux(zs, m).wait_send()
+            for xs in range(2):
+                go_core(zs, xs, m).wait_send()
+    for d in range(1, 8):
+        level_copy(d).wait_send()
+
+    total = energy[occ]
+    for d in range(1, 16):
+        out_copy(d).wait_recv()
+        total = total + shares[d]
+    out_ref[...] = jnp.where(x == 0, total[0:2, 0:8], total[0:2, 8:16])
+    for d in range(1, 16):
+        out_copy(d).wait_send()
+
+
+def fused_body(raw_ints, kept, eps_occ, eps_vir, metric_factor):
+    bf, dma = jnp.bfloat16, pltpu.SemaphoreType.DMA
+    vir = eps_vir.astype(F32)
+    occ_tile = jnp.broadcast_to(jnp.tile(eps_occ.astype(F32), 4)[:, None], (8, 128))
+    vmem = pl.BlockSpec(memory_space=pltpu.VMEM)
+    return pl.pallas_call(
+        kernel,
+        out_shape=jax.ShapeDtypeStruct((2, 8), F32),
+        in_specs=[vmem, pl.BlockSpec(memory_space=pltpu.SMEM), vmem, vmem, vmem, vmem],
+        out_specs=vmem,
+        scratch_shapes=[
+            pltpu.VMEM((4, 2, 2, 4, 2, 128, 128), bf),
+            pltpu.VMEM((512, 512), bf),
+            pltpu.VMEM((8, 256, 512), bf),
+            pltpu.VMEM((256, 256), F32),
+            pltpu.VMEM((8, 8, 128), F32),
+            pltpu.VMEM((8, 8, 128), F32),
+            pltpu.VMEM((16, 8, 128), F32),
+            dma((4, 2, 2, 4)),
+            dma((4, 4)),
+            dma((4, 4)),
+            dma((4, 2)),
+            dma((4, 2, 2)),
+            dma((8,)),
+            dma((8,)),
+            dma((16,)),
+            dma((16,)),
+        ],
+        compiler_params=pltpu.CompilerParams(
+            collective_id=0, has_side_effects=True, vmem_limit_bytes=40 * 2**20
+        ),
+    )(raw_ints, kept, occ_tile, vir[None, :], vir[:, None], metric_factor)
 
 
 def pair_terms(
@@ -85,4 +371,12 @@
         P(),
     )
     out_specs = P(("parts", "occ"), "aux")
-    return jax.shard_map(body, mesh=mesh, in_specs=in_specs, out_specs=out_specs, check_vma=False)
+    fits = mesh.shape["occ"] == 8 and mesh.shape["aux"] == 2
+
+    def step(raw_ints, kept, eps_occ, eps_vir, metric_factor):
+        sizes = (raw_ints.shape, kept.shape, eps_occ.shape, eps_vir.shape)
+        fused = fits and sizes == ((16, 128, 64), (8, 4, 4), (2,), (256,))
+        run = fused_body if fused else body
+        return run(raw_ints, kept, eps_occ, eps_vir, metric_factor)
+
+    return jax.shard_map(step, mesh=mesh, in_specs=in_specs, out_specs=out_specs, check_vma=False)

time: 124 us -> 41.2 us (0.33)
  blocking collectives: 43.8 us -> 0 us
  Pallas kernels: 0 us -> 36.7 us
  waiting for transfers between devices: 29.5 us -> 0 us
  matrix products: 23.9 us -> 0 us
  between operations: 14.8 us -> 0.03 us
  local copies, waits for them, and re-layouts: 7.17 us -> 3.54 us
  other arithmetic: 3.58 us -> 0.72 us
    pallas_call x0 -> x1, Pallas kernels: none -> 36.7 us  [fused_body(): pl.pallas_call(kernel, out_shape=jax.ShapeDtypeStruct((2, 8), F32), in_sp...]
    all_gather x1 -> x0, waiting for transfers between devices: 29.5 us -> none  [body(): partner_rows = lax.all_gather(own_full, 'occ', axis=0, tiled=True)]
    dot_general x17 -> x0, matrix products: 23.9 us -> none  [the longest x8 12.6 us: pair_terms(): jnp.einsum('ibp,jap->iajb', left_cols, right_slice, preferred_element_typ...]
    unnamed x2 -> x0, blocking collectives: 19.5 us -> none
    all_to_all x1 -> x0, blocking collectives: 15.9 us -> none  [body(): lax.all_to_all(screened, 'occ', split_axis=0, concat_axis=2, tiled=True)]
    all_gather x1 -> x0, blocking collectives: 8.46 us -> none  [body(): own_full = lax.all_gather(own_slice, 'aux', axis=1, tiled=True)]
    dynamic_update_slice x16 -> x0, local copies, waits for them, and re-layouts: 2.16 us -> none  [add_block(): return lax.dynamic_update_slice_in_dim(totals, before + term, column, 1)]
    dynamic_slice x18 -> x0, local copies, waits for them, and re-layouts: 1.46 us -> none  [the longest x16 1.37 us: add_block(): before = lax.dynamic_slice_in_dim(totals, column, own_occ, 1)]
  transfers between devices with their start and end apart: 1 -> 0, of which waited for: 1 -> 0; matrix products, arithmetic and copies ran while one was open for 1% -> 0% of each run, Pallas kernels for 0% -> 0%
where the time goes in v1:
time: 41.2 us; the launch traced here: 41 us
  Pallas kernels  36.7 us (89%)
  local copies, waits for them, and re-layouts  3.54 us (9%)
  other arithmetic  0.72 us (2%)
    pallas_call x1, Pallas kernels, fused_body(): pl.pallas_call(kernel, out_shape=jax.ShapeDtypeStruct((2, 8), F32), in_sp...  36.7 us
    unnamed x5, local copies, waits for them, and re-layouts  2.59 us

profile of v1, /device:TPU:0, one launch (start us, length us, event | category | flops | bytes accessed | tf_op | source)
XLA Modules:
  0.0 41.0 jit_solution(7242539584677615054)
XLA Ops:
  0.0 0.0 copy-start
  0.0 0.7 %convert_element_type.7 = f32[256]{0:T(256)S(1)} convert(bf16[256]{0:T(256)(128)(2,1)} %param.8) | non-fusion elementwise | flops 256 | bytes 1536 | tf_op jit(solution)/shard_map/convert_element_type | solution.py:264
  0.7 0.7 %tile.2 = f32[4,2]{1,0:T(4,128)S(1)} broadcast(bf16[2]{0:T(256)(128)(2,1)} %param.7), dimensions={1} | broadcast | bytes 36 | tf_op jit(solution)/shard_map/tile | solution.py:265
  1.4 0.1 broadcast_in_dim.13
  1.5 0.1 broadcast_in_dim.14.occ_ref
  1.5 0.8 %copy.9.kept_ref = s32[8,4,4]{2,1,0:T(4,128)S(1)} copy(s32[8,4,4]{0,2,1:T(4,128)} %param.6) | data formatting | bytes 1024 | tf_op args[1]
  2.3 0.1 copy.10.col_ref
  2.5 1.2 %copy.8.raw_ref = bf16[16,128,64]{2,1,0:T(8,128)(2,1)S(1)} copy(bf16[16,128,64]{1,2,0:T(8,128)(2,1)} %param.5) | data formatting | bytes 524288 | tf_op args[0]
  3.7 0.0 copy-done
  3.7 36.7 %shard_map.55 = f32[2,8]{1,0:T(2,128)S(1)} custom-call(bf16[16,128,64]{2,1,0:T(8,128)(2,1)S(1)} %copy.8.raw_ref, s32[8,4,4]{2,1,0:T(4,128)S(1)} %copy.9.kept_ref, f32[8,128]{1,0:T(8,128)S(1)} %broadcast_in_dim.14.occ_ref, f32[1,256]{1,0:T(1,128)S(1)} %bitcast.3, f32[256,1]{1,0:T(8,128)S(1)} %copy.10.col_ref, bf16[512,512]{1,0:T(8,128)(2,1)S(1)} %copy-done), custom_call_target="tpu_custom_call" | custom-call | tf_op jit(solution)/shard_map/pallas_call | solution.py:267
  40.4 0.6 %copy.12 = f32[2,8]{1,0:T(2,128)} copy(f32[2,8]{1,0:T(2,128)S(1)} %shard_map.55) | data formatting | bytes 128
Async XLA Ops:
  0.0 3.7 %copy-start = (bf16[512,512]{1,0:T(8,128)(2,1)S(1)}, bf16[512,512]{1,0:T(8,128)(2,1)}, u32[]{:S(2)}) copy-start(bf16[512,512]{1,0:T(8,128)(2,1)} %metric_ref.1) | copy-start | bytes 1572868

commit v2 on v1

--- a/solution.py
+++ b/solution.py
@@ -1,5 +1,3 @@
-import functools
-
 import jax
 import jax.numpy as jnp
 from jax import lax
@@ -20,8 +18,8 @@
 
 
 def kernel(
-    raw_ref, kept_ref, occ_ref, row_ref, col_ref, metric_ref, out_ref,
-    blocks, mat, fac, base, levels, energy, shares,
+    raw_ref, kept_ref, occ_ref, vir_ref, metric_ref, out_ref,
+    blocks, mat, fac, base, levels, energy, shares, gathered,
     recv, s_right, s_left, s_aux, s_core, s_lev, r_lev, s_out, r_out,
 ):
     occ = lax.axis_index("occ")
@@ -40,13 +38,16 @@
             barrier, inc=1, device_id={"occ": peer // 2, "aux": peer % 2}, device_id_type=MESH
         )
 
-    lane = lax.broadcasted_iota(jnp.int32, (2 * VB, 2 * VB), 1) % VB + c * VB
-    row = lax.broadcasted_iota(jnp.int32, (2 * VB, 2 * VB), 0)
+    place = lax.broadcasted_iota(jnp.int32, (VB, 2 * VB), 0) + c * VB
+    lane = lax.broadcasted_iota(jnp.int32, (VB, 2 * VB), 1)
     for k in range(8):
-        both = jnp.concatenate([raw_ref[2 * k], raw_ref[2 * k + 1]], axis=1).astype(F32)
-        limit = jnp.where(row < VB, kept_ref[k, 2 * x, z], kept_ref[k, 2 * x + 1, z])
-        blocks[z, x, c, k // 2, k % 2] = jnp.where(lane < limit, both, 0.0).astype(jnp.bfloat16)
-    levels[occ] = occ_ref[...]
+        limit = jnp.where(lane < VB, kept_ref[2 * x, z, k], kept_ref[2 * x + 1, z, k])
+        for i in (2 * k, 2 * k + 1):
+            kept_part = jnp.where(place < limit, raw_ref[i].astype(F32), 0.0)
+            blocks[z, x, c, i // 4, i % 4] = kept_part.astype(jnp.bfloat16)
+    pair = occ_ref[...].astype(F32)
+    row8 = lax.broadcasted_iota(jnp.int32, (8, 128), 0)
+    levels[occ] = jnp.where(row8 == 0, pair[:, 0:1], pair[:, 1:2])
 
     pl.semaphore_wait(barrier, 15)
 
@@ -91,9 +92,9 @@
             go_core(zs, 1 - x, m).start()
 
     for n in range(4):
-        @pl.when((z < 3) & (n >= z))
-        def _():
-            go_right(z, n).start()
+        @pl.when((z < 3) & (3 - n >= z))
+        def _():
+            go_right(z, 3 - n).start()
 
         @pl.when((z > 0) & (n < left_lim))
         def _():
@@ -118,14 +119,15 @@
 
     for d in range(1, 8):
         level_copy(d).start()
-    base[...] = col_ref[...] + row_ref[...]
+    across = jnp.broadcast_to(vir_ref[...].astype(F32), (256, 256))
+    base[...] = across + across.T
     energy[...] = jnp.zeros_like(energy)
 
     for t in range(1, 4):
         @pl.when(z >= t)
         def _():
             zs = jnp.maximum(z - t, 0)
-            for n in range(4):
+            for n in (3, 2, 1, 0):
                 @pl.when(n >= z - 1)
                 def _():
                     arrived(zs, x, c, n)
@@ -183,18 +185,16 @@
         @pl.when((diag & (kk // 2 == c)) | (jnp.logical_not(diag) & ((kk == c) | (kk >= 2))))
         def _():
             n = own[kk // 2]
-            for xs in range(2):
-                for zs in range(4):
-                    t0 = blocks[zs, xs, 0, n, kk % 2]
-                    t1 = blocks[zs, xs, 1, n, kk % 2]
-                    mat[pl.ds(xs * 128, 128), pl.ds(zs * 128, 128)] = jnp.concatenate(
-                        [t0[:, :VB], t1[:, :VB]], axis=1)
-                    mat[pl.ds(256 + xs * 128, 128), pl.ds(zs * 128, 128)] = jnp.concatenate(
-                        [t0[:, VB:], t1[:, VB:]], axis=1)
-            prod = jnp.dot(mat[...], metric_ref[...], preferred_element_type=F32)
-            prod = prod.astype(jnp.bfloat16)
-            fac[2 * kk] = prod[:256]
-            fac[2 * kk + 1] = prod[256:]
+            for o in range(2):
+                for xs in range(2):
+                    for zs in range(4):
+                        for cs in range(2):
+                            mat[pl.ds(zs * 128 + cs * 64, 64), pl.ds(xs * 128, 128)] = blocks[
+                                zs, xs, cs, n, 2 * (kk % 2) + o]
+                prod = lax.dot_general(
+                    mat[...], metric_ref[...], (((0,), (0,)), ((), ())),
+                    preferred_element_type=F32)
+                fac[2 * kk + o] = prod.astype(jnp.bfloat16)
 
     for d in range(1, 8):
         level_wait(d)
@@ -215,23 +215,31 @@
         pair_level = jnp.concatenate([pair_level, pair_level], axis=1)
         term = direct * (2.0 * direct - swapped) / (base[...] - pair_level)
         term = -jnp.sum(jnp.sum(term, axis=0, keepdims=True), axis=1, keepdims=True)
-        energy[gi // 2] += jnp.where((rows8 == gi % 2) & (lanes8 == gj), term, 0.0)
-        turned = (rows8 == gj % 2) & (lanes8 == gi) & (gi != gj)
-        energy[gj // 2] += jnp.where(turned, term, 0.0)
+        upper = (rows8 == gi % 2) & (lanes8 == gj % 8)
+        energy[li // 2] += jnp.where(upper, term, 0.0)
+        turned = (rows8 == gj % 2) & (lanes8 == gi % 8) & (gi != gj)
+        energy[lj // 2] += jnp.where(turned, term, 0.0)
         return carry
 
     lax.fori_loop(0, jnp.where(diag, 10, 8), one_pair, 0)
 
-    def out_copy(d):
-        to = (me + d) % 16
+    used = [jnp.logical_not(diag) | (c == h // 2) for h in range(4)]
+    owner_occ = [2 * own[h // 2] + h % 2 for h in range(4)]
+    column = [jnp.where(diag, own[h // 2], own[1 - h // 2]) for h in range(4)]
+    slot = [column[h] % 2 * 2 + jnp.where(diag, 0, c) for h in range(4)]
+    to_self = [(owner_occ[h] == occ) & (column[h] // 2 == x) for h in range(4)]
+
+    def out_copy(h):
         return pltpu.make_async_remote_copy(
-            src_ref=energy.at[to // 2], dst_ref=shares.at[d],
-            send_sem=s_out.at[d], recv_sem=r_out.at[d],
-            device_id={"occ": to // 2, "aux": to % 2}, device_id_type=MESH,
+            src_ref=energy.at[h], dst_ref=shares.at[slot[h]],
+            send_sem=s_out.at[h], recv_sem=r_out.at[slot[h]],
+            device_id={"occ": owner_occ[h], "aux": column[h] // 2}, device_id_type=MESH,
         )
 
-    for d in range(1, 16):
-        out_copy(d).start()
+    for h in range(4):
+        @pl.when(used[h] & jnp.logical_not(to_self[h]))
+        def _():
+            out_copy(h).start()
 
     for n in range(4):
         for t in range(4):
@@ -250,33 +258,50 @@
     for d in range(1, 8):
         level_copy(d).wait_send()
 
-    total = energy[occ]
-    for d in range(1, 16):
-        out_copy(d).wait_recv()
-        total = total + shares[d]
-    out_ref[...] = jnp.where(x == 0, total[0:2, 0:8], total[0:2, 8:16])
-    for d in range(1, 16):
-        out_copy(d).wait_send()
+    gathered[...] = jnp.zeros_like(gathered)
+    for h in range(4):
+        @pl.when(used[h] & to_self[h])
+        def _():
+            gathered[...] += energy[h]
+    for kk in range(2):
+        for cs in range(2):
+            col = 2 * x + kk
+            off_self = ((own[0] == z) & (own[1] == col)) | ((own[1] == z) & (own[0] == col))
+            diag_self = (col == z) & (jnp.where(c == 0, own[0], own[1]) == z)
+            mine = jnp.where(diag, diag_self, off_self & (cs == c))
+
+            @pl.when(((col != z) | (cs == 0)) & jnp.logical_not(mine))
+            def _():
+                pltpu.make_async_remote_copy(
+                    src_ref=energy.at[0], dst_ref=shares.at[2 * kk + cs],
+                    send_sem=s_out.at[0], recv_sem=r_out.at[2 * kk + cs],
+                    device_id={"occ": core_id}, device_id_type=MESH,
+                ).wait_recv()
+                gathered[...] += shares[2 * kk + cs]
+    out_ref[...] = gathered[0:2, 0:8]
+    for h in range(4):
+        @pl.when(used[h] & jnp.logical_not(to_self[h]))
+        def _():
+            out_copy(h).wait_send()
 
 
 def fused_body(raw_ints, kept, eps_occ, eps_vir, metric_factor):
     bf, dma = jnp.bfloat16, pltpu.SemaphoreType.DMA
-    vir = eps_vir.astype(F32)
-    occ_tile = jnp.broadcast_to(jnp.tile(eps_occ.astype(F32), 4)[:, None], (8, 128))
     vmem = pl.BlockSpec(memory_space=pltpu.VMEM)
     return pl.pallas_call(
         kernel,
         out_shape=jax.ShapeDtypeStruct((2, 8), F32),
-        in_specs=[vmem, pl.BlockSpec(memory_space=pltpu.SMEM), vmem, vmem, vmem, vmem],
+        in_specs=[vmem, pl.BlockSpec(memory_space=pltpu.SMEM), vmem, vmem, vmem],
         out_specs=vmem,
         scratch_shapes=[
-            pltpu.VMEM((4, 2, 2, 4, 2, 128, 128), bf),
-            pltpu.VMEM((512, 512), bf),
+            pltpu.VMEM((4, 2, 2, 4, 4, 64, 128), bf),
+            pltpu.VMEM((512, 256), bf),
             pltpu.VMEM((8, 256, 512), bf),
             pltpu.VMEM((256, 256), F32),
             pltpu.VMEM((8, 8, 128), F32),
-            pltpu.VMEM((8, 8, 128), F32),
-            pltpu.VMEM((16, 8, 128), F32),
+            pltpu.VMEM((4, 8, 128), F32),
+            pltpu.VMEM((4, 8, 128), F32),
+            pltpu.VMEM((8, 128), F32),
             dma((4, 2, 2, 4)),
             dma((4, 4)),
             dma((4, 4)),
@@ -284,13 +309,16 @@
             dma((4, 2, 2)),
             dma((8,)),
             dma((8,)),
-            dma((16,)),
-            dma((16,)),
+            dma((4,)),
+            dma((4,)),
         ],
         compiler_params=pltpu.CompilerParams(
             collective_id=0, has_side_effects=True, vmem_limit_bytes=40 * 2**20
         ),
-    )(raw_ints, kept, occ_tile, vir[None, :], vir[:, None], metric_factor)
+    )(
+        raw_ints.transpose(0, 2, 1), kept.transpose(1, 2, 0), eps_occ[None], eps_vir[None],
+        metric_factor,
+    )
 
 
 def pair_terms(

time: 41.2 us -> 40.5 us (0.983)
  Pallas kernels: 36.7 us -> 35.6 us
  local copies, waits for them, and re-layouts: 3.54 us -> 4.56 us
  other arithmetic: 0.72 us -> 0 us
    unnamed x5 -> x11, local copies, waits for them, and re-layouts: 2.59 us -> 4.56 us
    pallas_call x1, Pallas kernels: 36.7 us -> 35.6 us  [fused_body(): pl.pallas_call(kernel, out_shape=jax.ShapeDtypeStruct((2, 8), F32), in_sp...]
    convert_element_type x1 -> x0, other arithmetic: 0.72 us -> none  [fused_body(): vir = eps_vir.astype(F32)]
    another operation x1 -> x0, local copies, waits for them, and re-layouts: 0.66 us -> none  [fused_body(): jnp.tile(eps_occ.astype(F32), 4)[:, None]]
where the time goes in v2:
time: 40.5 us; the launch traced here: 40.2 us
  Pallas kernels  35.6 us (88%)
  local copies, waits for them, and re-layouts  4.56 us (11%)
    pallas_call x1, Pallas kernels, fused_body(): pl.pallas_call(kernel, out_shape=jax.ShapeDtypeStruct((2, 8), F32), in_sp...  35.6 us
    unnamed x11, local copies, waits for them, and re-layouts  4.56 us

profile of v2, /device:TPU:0, one launch (start us, length us, event | category | flops | bytes accessed | tf_op | source)
XLA Modules:
  0.0 40.2 jit_solution(3964729821558053268)
XLA Ops:
  0.0 0.0 copy-start.4
  0.0 0.7 %copy-done.4 = bf16[256]{0:T(256)(128)(2,1)S(1)} copy-done((bf16[256]{0:T(256)(128)(2,1)S(1)}, bf16[256]{0:T(256)(128)(2,1)}, u32[]{:S(2)}) %copy-start.4) | copy-done | bytes 536
  0.7 0.0 copy-start.3
  0.7 0.6 %copy-done.3 = bf16[2]{0:T(256)(128)(2,1)S(1)} copy-done((bf16[2]{0:T(256)(128)(2,1)S(1)}, bf16[2]{0:T(256)(128)(2,1)}, u32[]{:S(2)}) %copy-start.3) | copy-done | bytes 28
  1.3 0.0 copy-start
  1.3 1.0 %copy-done = bf16[512,512]{1,0:T(8,128)(2,1)S(1)} copy-done((bf16[512,512]{1,0:T(8,128)(2,1)S(1)}, bf16[512,512]{1,0:T(8,128)(2,1)}, u32[]{:S(2)}) %copy-start) | copy-done | bytes 524312
  2.4 0.0 copy-start.1
  2.4 0.9 %copy-done.1 = bf16[16,128,64]{1,2,0:T(8,128)(2,1)S(1)} copy-done((bf16[16,128,64]{1,2,0:T(8,128)(2,1)S(1)}, bf16[16,128,64]{1,2,0:T(8,128)(2,1)}, u32[]{:S(2)}) %copy-start.1) | copy-done | bytes 262168
  3.3 0.0 copy-start.2
  3.3 0.7 %copy-done.2 = s32[8,4,4]{0,2,1:T(4,128)S(1)} copy-done((s32[8,4,4]{0,2,1:T(4,128)S(1)}, s32[8,4,4]{0,2,1:T(4,128)}, u32[]{:S(2)}) %copy-start.2) | copy-done | bytes 536
  4.0 35.6 %shard_map.55 = f32[2,8]{1,0:T(2,128)S(1)} custom-call(bf16[16,64,128]{2,1,0:T(8,128)(2,1)S(1)} %bitcast.3, s32[4,4,8]{2,1,0:T(4,128)S(1)} %bitcast.4, bf16[1,2]{1,0:T(2,128)(2,1)S(1)} %bitcast.5, bf16[1,256]{1,0:T(2,128)(2,1)S(1)} %broadcast_in_dim.7.vir_ref, bf16[512,512]{1,0:T(8,128)(2,1)S(1)} %copy-done), custom_call_target="tpu_custom_call" | custom-call | tf_op jit(solution)/shard_map/pallas_call | solution.py:291
  39.6 0.6 %copy.7 = f32[2,8]{1,0:T(2,128)} copy(f32[2,8]{1,0:T(2,128)S(1)} %shard_map.55) | data formatting | bytes 128
  (1 shorter events, 0.0 us)
Async XLA Ops:
  0.0 0.7 %copy-start.4 = (bf16[256]{0:T(256)(128)(2,1)S(1)}, bf16[256]{0:T(256)(128)(2,1)}, u32[]{:S(2)}) copy-start(bf16[256]{0:T(256)(128)(2,1)} %param.8) | copy-start | bytes 1540
  0.7 0.7 %copy-start.3 = (bf16[2]{0:T(256)(128)(2,1)S(1)}, bf16[2]{0:T(256)(128)(2,1)}, u32[]{:S(2)}) copy-start(bf16[2]{0:T(256)(128)(2,1)} %param.7) | copy-start | bytes 16
  1.3 1.0 %copy-start = (bf16[512,512]{1,0:T(8,128)(2,1)S(1)}, bf16[512,512]{1,0:T(8,128)(2,1)}, u32[]{:S(2)}) copy-start(bf16[512,512]{1,0:T(8,128)(2,1)} %metric_ref.1) | copy-start | bytes 1572868
  2.4 0.9 %copy-start.1 = (bf16[16,128,64]{1,2,0:T(8,128)(2,1)S(1)}, bf16[16,128,64]{1,2,0:T(8,128)(2,1)}, u32[]{:S(2)}) copy-start(bf16[16,128,64]{1,2,0:T(8,128)(2,1)} %param.5) | copy-start | bytes 786436
  3.3 0.7 %copy-start.2 = (s32[8,4,4]{0,2,1:T(4,128)S(1)}, s32[8,4,4]{0,2,1:T(4,128)}, u32[]{:S(2)}) copy-start(s32[8,4,4]{0,2,1:T(4,128)} %param.6) | copy-start | bytes 1540

commit v3 on v2

--- a/solution.py
+++ b/solution.py
@@ -18,9 +18,10 @@
 
 
 def kernel(
-    raw_ref, kept_ref, occ_ref, vir_ref, metric_ref, out_ref,
+    raw_hbm, kept_hbm, occ_hbm, vir_hbm, metric_hbm, out_ref,
+    raw_ref, kept_ref, occ_ref, vir_ref, metric_ref,
     blocks, mat, fac, base, levels, energy, shares, gathered,
-    recv, s_right, s_left, s_aux, s_core, s_lev, r_lev, s_out, r_out,
+    fetch, recv, s_right, s_left, s_aux, s_core, s_lev, r_lev, s_out, r_out,
 ):
     occ = lax.axis_index("occ")
     x = lax.axis_index("aux")
@@ -31,6 +32,15 @@
     own = needs(x, z)
     other = needs(1 - x, z)
 
+    fetches = [
+        pltpu.make_async_copy(src, dst, fetch.at[k])
+        for k, (src, dst) in enumerate([
+            (raw_hbm, raw_ref), (kept_hbm, kept_ref), (occ_hbm, occ_ref),
+            (vir_hbm, vir_ref), (metric_hbm, metric_ref),
+        ])
+    ]
+    for one in fetches:
+        one.start()
     barrier = pltpu.get_barrier_semaphore()
     for d in range(1, 16):
         peer = (me + d) % 16
@@ -38,6 +48,8 @@
             barrier, inc=1, device_id={"occ": peer // 2, "aux": peer % 2}, device_id_type=MESH
         )
 
+    for one in fetches[:3]:
+        one.wait()
     place = lax.broadcasted_iota(jnp.int32, (VB, 2 * VB), 0) + c * VB
     lane = lax.broadcasted_iota(jnp.int32, (VB, 2 * VB), 1)
     for k in range(8):
@@ -71,35 +83,47 @@
     def go_left(zs, n):
         return copy(zs, x, c, n, s_left.at[zs, n], left_id, x)
 
-    def go_aux(zs, m):
-        return copy(zs, x, c, other[m], s_aux.at[zs, m], occ, 1 - x)
-
-    def go_core(zs, xs, m):
-        return copy(zs, xs, c, own[m], s_core.at[zs, xs, m], core_id, x)
+    def go_aux(zs, n):
+        return copy(zs, x, c, n, s_aux.at[zs, n], occ, 1 - x)
+
+    def go_core(zs, xs, n):
+        return copy(zs, xs, c, n, s_core.at[zs, xs, n], core_id, x)
 
     def arrived(zs, xs, cs, n):
         copy(zs, xs, cs, n, s_right.at[0, 0], core_id, x).wait_recv()
 
-    def spread(zs):
-        for m in range(2):
-            go_aux(zs, m).start()
-        for m in range(2):
-            go_core(zs, x, m).start()
+    def among(n, pair_of):
+        return (n == pair_of[0]) | (n == pair_of[1])
+
+    def spread(zs, n):
+        @pl.when(among(n, other))
+        def _():
+            go_aux(zs, n).start()
+
+        @pl.when(among(n, own))
+        def _():
+            go_core(zs, x, n).start()
 
     def take_aux(zs):
         for m in range(2):
             arrived(zs, 1 - x, c, own[m])
-            go_core(zs, 1 - x, m).start()
+            go_core(zs, 1 - x, own[m]).start()
+
+    def send_right(zs, n):
+        @pl.when((z < 3) & (n >= z))
+        def _():
+            go_right(zs, n).start()
+
+    def send_left(zs, n):
+        @pl.when((z > 0) & (n < left_lim))
+        def _():
+            go_left(zs, n).start()
 
     for n in range(4):
-        @pl.when((z < 3) & (3 - n >= z))
-        def _():
-            go_right(z, 3 - n).start()
-
-        @pl.when((z > 0) & (n < left_lim))
-        def _():
-            go_left(z, n).start()
-    spread(z)
+        send_right(z, 3 - n)
+        send_left(z, n)
+    for n in range(4):
+        spread(z, n)
 
     def level_copy(d):
         to = (occ + d) % 8
@@ -119,42 +143,27 @@
 
     for d in range(1, 8):
         level_copy(d).start()
-    across = jnp.broadcast_to(vir_ref[...].astype(F32), (256, 256))
+    fetches[3].wait()
+    fetches[4].wait()
+    across = jnp.broadcast_to(vir_ref[...].astype(F32)[None], (256, 256))
     base[...] = across + across.T
     energy[...] = jnp.zeros_like(energy)
 
     for t in range(1, 4):
-        @pl.when(z >= t)
-        def _():
-            zs = jnp.maximum(z - t, 0)
-            for n in (3, 2, 1, 0):
-                @pl.when(n >= z - 1)
-                def _():
-                    arrived(zs, x, c, n)
-
-                @pl.when((z < 3) & (n >= z))
-                def _():
-                    go_right(zs, n).start()
-
-        @pl.when(z + t <= 3)
-        def _():
-            zs = jnp.minimum(z + t, 3)
-            for n in range(4):
-                @pl.when(n < left_lim_in)
-                def _():
-                    arrived(zs, x, c, n)
-
-                @pl.when((z > 0) & (n < left_lim))
-                def _():
-                    go_left(zs, n).start()
-
-        @pl.when(z >= t)
-        def _():
-            spread(jnp.maximum(z - t, 0))
-
-        @pl.when(z + t <= 3)
-        def _():
-            spread(jnp.minimum(z + t, 3))
+        for step in range(4):
+            @pl.when((z >= t) & (3 - step >= z - 1))
+            def _():
+                zs = jnp.maximum(z - t, 0)
+                arrived(zs, x, c, 3 - step)
+                send_right(zs, 3 - step)
+                spread(zs, 3 - step)
+
+            @pl.when((z + t <= 3) & (step < left_lim_in))
+            def _():
+                zs = jnp.minimum(z + t, 3)
+                arrived(zs, x, c, step)
+                send_left(zs, step)
+                spread(zs, step)
 
         if t == 1:
             take_aux(z)
@@ -202,7 +211,7 @@
     rows8 = lax.broadcasted_iota(jnp.int32, (8, 128), 0)
     lanes8 = lax.broadcasted_iota(jnp.int32, (8, 128), 1)
 
-    def one_pair(t, carry):
+    def one_pair(t):
         li = jnp.where(diag, 4 * c + t % 4, 2 * c + t // 4)
         lj = jnp.where(diag, 4 * c + (t % 4 + t // 4) % 4, 4 + t % 4)
         gi = 4 * jnp.where(li < 4, own[0], own[1]) + li % 4
@@ -219,9 +228,13 @@
         energy[li // 2] += jnp.where(upper, term, 0.0)
         turned = (rows8 == gj % 2) & (lanes8 == gi % 8) & (gi != gj)
         energy[lj // 2] += jnp.where(turned, term, 0.0)
+
+    def two_pairs(t, carry):
+        one_pair(2 * t)
+        one_pair(2 * t + 1)
         return carry
 
-    lax.fori_loop(0, jnp.where(diag, 10, 8), one_pair, 0)
+    lax.fori_loop(0, jnp.where(diag, 5, 4), two_pairs, 0)
 
     used = [jnp.logical_not(diag) | (c == h // 2) for h in range(4)]
     owner_occ = [2 * own[h // 2] + h % 2 for h in range(4)]
@@ -252,9 +265,9 @@
                 go_left(jnp.minimum(z + t, 3), n).wait_send()
     for zs in range(4):
         for m in range(2):
-            go_aux(zs, m).wait_send()
+            go_aux(zs, other[m]).wait_send()
             for xs in range(2):
-                go_core(zs, xs, m).wait_send()
+                go_core(zs, xs, own[m]).wait_send()
     for d in range(1, 8):
         level_copy(d).wait_send()
 
@@ -291,9 +304,14 @@
     return pl.pallas_call(
         kernel,
         out_shape=jax.ShapeDtypeStruct((2, 8), F32),
-        in_specs=[vmem, pl.BlockSpec(memory_space=pltpu.SMEM), vmem, vmem, vmem],
+        in_specs=[pl.BlockSpec(memory_space=pl.ANY)] * 5,
         out_specs=vmem,
         scratch_shapes=[
+            pltpu.VMEM((16, 64, 128), bf),
+            pltpu.SMEM((4, 4, 8), jnp.int32),
+            pltpu.VMEM((1, 2), bf),
+            pltpu.VMEM((256,), bf),
+            pltpu.VMEM((512, 512), bf),
             pltpu.VMEM((4, 2, 2, 4, 4, 64, 128), bf),
             pltpu.VMEM((512, 256), bf),
             pltpu.VMEM((8, 256, 512), bf),
@@ -302,21 +320,22 @@
             pltpu.VMEM((4, 8, 128), F32),
             pltpu.VMEM((4, 8, 128), F32),
             pltpu.VMEM((8, 128), F32),
+            dma((5,)),
             dma((4, 2, 2, 4)),
             dma((4, 4)),
             dma((4, 4)),
-            dma((4, 2)),
-            dma((4, 2, 2)),
+            dma((4, 4)),
+            dma((4, 2, 4)),
             dma((8,)),
             dma((8,)),
             dma((4,)),
             dma((4,)),
         ],
         compiler_params=pltpu.CompilerParams(
-            collective_id=0, has_side_effects=True, vmem_limit_bytes=40 * 2**20
+            collective_id=0, has_side_effects=True, vmem_limit_bytes=60 * 2**20
         ),
     )(
-        raw_ints.transpose(0, 2, 1), kept.transpose(1, 2, 0), eps_occ[None], eps_vir[None],
+        raw_ints.transpose(0, 2, 1), kept.transpose(1, 2, 0), eps_occ[None], eps_vir,
         metric_factor,
     )
 

time: 40.5 us -> 33.7 us (0.83)
  Pallas kernels: 35.6 us -> 32.2 us
  local copies, waits for them, and re-layouts: 4.56 us -> 1.24 us
    pallas_call x1, Pallas kernels: 35.6 us -> 32.2 us  [fused_body(): pl.pallas_call(kernel, out_shape=jax.ShapeDtypeStruct((2, 8), F32), in_sp...]
    unnamed x11 -> x1, local copies, waits for them, and re-layouts: 4.56 us -> 1.24 us
where the time goes in v3:
time: 33.7 us; the launch traced here: 33.5 us
  Pallas kernels  32.2 us (96%)
  local copies, waits for them, and re-layouts  1.24 us (4%)
    pallas_call x1, Pallas kernels, fused_body(): pl.pallas_call(kernel, out_shape=jax.ShapeDtypeStruct((2, 8), F32), in_sp...  32.2 us
    unnamed x1, local copies, waits for them, and re-layouts  1.24 us

profile of v3, /device:TPU:0, one launch (start us, length us, event | category | flops | bytes accessed | tf_op | source)
XLA Modules:
  0.0 33.5 jit_solution(1525362721114310359)
XLA Ops:
  0.0 32.2 %shard_map.55 = f32[2,8]{1,0:T(2,128)} custom-call(bf16[16,64,128]{2,1,0:T(8,128)(2,1)} %bitcast.3, s32[4,4,8]{2,1,0:T(4,128)} %bitcast.4, bf16[1,2]{1,0:T(2,128)(2,1)} %bitcast.5, bf16[256]{0:T(256)(128)(2,1)} %vir_hbm.1, bf16[512,512]{1,0:T(8,128)(2,1)} %metric_hbm.1), custom_call_target="tpu_custom_call" | custom-call | tf_op jit(solution)/shard_map/pallas_call | solution.py:304
  32.3 1.2 %copy.7 = f32[2,8]{1,0:T(2,128)} copy(f32[2,8]{1,0:T(2,128)} %shard_map.55) | data formatting | bytes 128

commit v4 on v3

--- a/solution.py
+++ b/solution.py
@@ -26,7 +26,6 @@
     occ = lax.axis_index("occ")
     x = lax.axis_index("aux")
     z, c = occ // 2, occ % 2
-    me = occ * 2 + x
     left_lim = jnp.where(z == 1, 2, 4)
     left_lim_in = jnp.where(z == 0, 2, 4)
     own = needs(x, z)
@@ -42,11 +41,25 @@
     for one in fetches:
         one.start()
     barrier = pltpu.get_barrier_semaphore()
-    for d in range(1, 16):
-        peer = (me + d) % 16
+    right_id = jnp.minimum(occ + 2, 7)
+    left_id = jnp.maximum(occ - 2, 0)
+    core_id = 2 * z + 1 - c
+
+    def greet(to_occ, to_x):
         pl.semaphore_signal(
-            barrier, inc=1, device_id={"occ": peer // 2, "aux": peer % 2}, device_id_type=MESH
+            barrier, inc=1, device_id={"occ": to_occ, "aux": to_x}, device_id_type=MESH
         )
+
+    greet(core_id, x)
+    greet(occ, 1 - x)
+
+    @pl.when(z < 3)
+    def _():
+        greet(right_id, x)
+
+    @pl.when(z > 0)
+    def _():
+        greet(left_id, x)
 
     for one in fetches[:3]:
         one.wait()
@@ -61,7 +74,7 @@
     row8 = lax.broadcasted_iota(jnp.int32, (8, 128), 0)
     levels[occ] = jnp.where(row8 == 0, pair[:, 0:1], pair[:, 1:2])
 
-    pl.semaphore_wait(barrier, 15)
+    pl.semaphore_wait(barrier, jnp.where((z == 0) | (z == 3), 3, 4))
 
     def copy(zs, xs, cs, n, send_sem, to_occ, to_x):
         return pltpu.make_async_remote_copy(
@@ -73,10 +86,6 @@
             device_id_type=MESH,
         )
 
-    right_id = jnp.minimum(occ + 2, 7)
-    left_id = jnp.maximum(occ - 2, 0)
-    core_id = 2 * z + 1 - c
-
     def go_right(zs, n):
         return copy(zs, x, c, n, s_right.at[zs, n], right_id, x)
 
@@ -119,30 +128,46 @@
         def _():
             go_left(zs, n).start()
 
+    def level_copy(zs, cs, send_sem, to_occ):
+        return pltpu.make_async_remote_copy(
+            src_ref=levels.at[2 * zs + cs], dst_ref=levels.at[2 * zs + cs],
+            send_sem=send_sem, recv_sem=r_lev.at[2 * zs + cs],
+            device_id={"occ": to_occ, "aux": x}, device_id_type=MESH,
+        )
+
+    def level_right(zs):
+        return level_copy(zs, c, s_lev.at[0, zs], right_id)
+
+    def level_left(zs):
+        return level_copy(zs, c, s_lev.at[1, zs], left_id)
+
+    def level_core(zs):
+        return level_copy(zs, c, s_lev.at[2, zs], core_id)
+
+    def level_arrived(zs, cs):
+        level_copy(zs, cs, s_lev.at[0, 0], core_id).wait_recv()
+
+    def pass_levels(zs, right, left):
+        if right:
+            @pl.when(z < 3)
+            def _():
+                level_right(zs).start()
+        if left:
+            @pl.when(z > 0)
+            def _():
+                level_left(zs).start()
+        level_core(zs).start()
+
+    pass_levels(z, True, True)
     for n in range(4):
         send_right(z, 3 - n)
-        send_left(z, n)
+
+        @pl.when((z != 2) | (n < 2))
+        def _():
+            send_left(z, n)
     for n in range(4):
         spread(z, n)
 
-    def level_copy(d):
-        to = (occ + d) % 8
-        return pltpu.make_async_remote_copy(
-            src_ref=levels.at[occ], dst_ref=levels.at[occ],
-            send_sem=s_lev.at[d], recv_sem=r_lev.at[d],
-            device_id={"occ": to}, device_id_type=MESH,
-        )
-
-    def level_wait(d):
-        frm = (occ + 8 - d) % 8
-        pltpu.make_async_remote_copy(
-            src_ref=levels.at[frm], dst_ref=levels.at[frm],
-            send_sem=s_lev.at[d], recv_sem=r_lev.at[d],
-            device_id={"occ": (occ + d) % 8}, device_id_type=MESH,
-        ).wait_recv()
-
-    for d in range(1, 8):
-        level_copy(d).start()
     fetches[3].wait()
     fetches[4].wait()
     across = jnp.broadcast_to(vir_ref[...].astype(F32)[None], (256, 256))
@@ -150,6 +175,16 @@
     energy[...] = jnp.zeros_like(energy)
 
     for t in range(1, 4):
+        @pl.when(z >= t)
+        def _():
+            level_arrived(jnp.maximum(z - t, 0), c)
+            pass_levels(jnp.maximum(z - t, 0), True, False)
+
+        @pl.when(z + t <= 3)
+        def _():
+            level_arrived(jnp.minimum(z + t, 3), c)
+            pass_levels(jnp.minimum(z + t, 3), False, True)
+
         for step in range(4):
             @pl.when((z >= t) & (3 - step >= z - 1))
             def _():
@@ -163,6 +198,11 @@
                 zs = jnp.minimum(z + t, 3)
                 arrived(zs, x, c, step)
                 send_left(zs, step)
+                if t == 1 and step == 1:
+                    @pl.when(z == 2)
+                    def _():
+                        send_left(z, 2)
+                        send_left(z, 3)
                 spread(zs, step)
 
         if t == 1:
@@ -205,8 +245,8 @@
                     preferred_element_type=F32)
                 fac[2 * kk + o] = prod.astype(jnp.bfloat16)
 
-    for d in range(1, 8):
-        level_wait(d)
+    for zs in range(4):
+        level_arrived(zs, 1 - c)
 
     rows8 = lax.broadcasted_iota(jnp.int32, (8, 128), 0)
     lanes8 = lax.broadcasted_iota(jnp.int32, (8, 128), 1)
@@ -268,8 +308,16 @@
             go_aux(zs, other[m]).wait_send()
             for xs in range(2):
                 go_core(zs, xs, own[m]).wait_send()
-    for d in range(1, 8):
-        level_copy(d).wait_send()
+    for t in range(4):
+        @pl.when((z >= t) & (z < 3))
+        def _():
+            level_right(jnp.maximum(z - t, 0)).wait_send()
+
+        @pl.when((z + t <= 3) & (z > 0))
+        def _():
+            level_left(jnp.minimum(z + t, 3)).wait_send()
+
+        level_core(t).wait_send()
 
     gathered[...] = jnp.zeros_like(gathered)
     for h in range(4):
@@ -326,7 +374,7 @@
             dma((4, 4)),
             dma((4, 4)),
             dma((4, 2, 4)),
-            dma((8,)),
+            dma((3, 4)),
             dma((8,)),
             dma((4,)),
             dma((4,)),

time: 33.7 us -> 33.8 us (level)
  no operation moved by 1% of the time
where the time goes in v4:
time: 33.8 us; the launch traced here: 33.6 us
  Pallas kernels  32.3 us (96%)
  local copies, waits for them, and re-layouts  1.24 us (4%)
    pallas_call x1, Pallas kernels, fused_body(): pl.pallas_call(kernel, out_shape=jax.ShapeDtypeStruct((2, 8), F32), in_sp...  32.3 us
    unnamed x1, local copies, waits for them, and re-layouts  1.24 us

profile of v4, /device:TPU:0, one launch (start us, length us, event | category | flops | bytes accessed | tf_op | source)
XLA Modules:
  0.0 33.6 jit_solution(4904953799523281157)
XLA Ops:
  0.0 32.3 %shard_map.55 = f32[2,8]{1,0:T(2,128)} custom-call(bf16[16,64,128]{2,1,0:T(8,128)(2,1)} %bitcast.3, s32[4,4,8]{2,1,0:T(4,128)} %bitcast.4, bf16[1,2]{1,0:T(2,128)(2,1)} %bitcast.5, bf16[256]{0:T(256)(128)(2,1)} %vir_hbm.1, bf16[512,512]{1,0:T(8,128)(2,1)} %metric_hbm.1), custom_call_target="tpu_custom_call" | custom-call | tf_op jit(solution)/shard_map/pallas_call | solution.py:352
  32.4 1.2 %copy.7 = f32[2,8]{1,0:T(2,128)} copy(f32[2,8]{1,0:T(2,128)} %shard_map.55) | data formatting | bytes 128

commit v5 on v4

--- a/solution.py
+++ b/solution.py
@@ -174,6 +174,11 @@
     base[...] = across + across.T
     energy[...] = jnp.zeros_like(energy)
 
+    def from_right(zs, n):
+        arrived(zs, x, c, n)
+        send_left(zs, n)
+        spread(zs, n)
+
     for t in range(1, 4):
         @pl.when(z >= t)
         def _():
@@ -193,17 +198,23 @@
                 send_right(zs, 3 - step)
                 spread(zs, 3 - step)
 
-            @pl.when((z + t <= 3) & (step < left_lim_in))
-            def _():
-                zs = jnp.minimum(z + t, 3)
-                arrived(zs, x, c, step)
-                send_left(zs, step)
+            late = (z == 1) & (step >= 2)
+
+            @pl.when((z + t <= 3) & (step < left_lim_in) & jnp.logical_not(late))
+            def _():
+                from_right(jnp.minimum(z + t, 3), step)
                 if t == 1 and step == 1:
                     @pl.when(z == 2)
                     def _():
                         send_left(z, 2)
                         send_left(z, 3)
-                spread(zs, step)
+
+        if t == 2:
+            @pl.when(z == 1)
+            def _():
+                for zs in (2, 3):
+                    for n in (2, 3):
+                        from_right(zs, n)
 
         if t == 1:
             take_aux(z)

time: 33.8 us -> 31 us (0.917)
  Pallas kernels: 32.3 us -> 29.6 us
    pallas_call x1, Pallas kernels: 32.3 us -> 29.6 us  [fused_body(): pl.pallas_call(kernel, out_shape=jax.ShapeDtypeStruct((2, 8), F32), in_sp...]
where the time goes in v5:
time: 31 us; the launch traced here: 30.8 us
  Pallas kernels  29.6 us (95%)
  local copies, waits for them, and re-layouts  1.24 us (4%)
    pallas_call x1, Pallas kernels, fused_body(): pl.pallas_call(kernel, out_shape=jax.ShapeDtypeStruct((2, 8), F32), in_sp...  29.6 us
    unnamed x1, local copies, waits for them, and re-layouts  1.24 us

profile of v5, /device:TPU:0, one launch (start us, length us, event | category | flops | bytes accessed | tf_op | source)
XLA Modules:
  0.0 30.8 jit_solution(12087147572457957685)
XLA Ops:
  0.0 29.6 %shard_map.55 = f32[2,8]{1,0:T(2,128)} custom-call(bf16[16,64,128]{2,1,0:T(8,128)(2,1)} %bitcast.3, s32[4,4,8]{2,1,0:T(4,128)} %bitcast.4, bf16[1,2]{1,0:T(2,128)(2,1)} %bitcast.5, bf16[256]{0:T(256)(128)(2,1)} %vir_hbm.1, bf16[512,512]{1,0:T(8,128)(2,1)} %metric_hbm.1), custom_call_target="tpu_custom_call" | custom-call | tf_op jit(solution)/shard_map/pallas_call | solution.py:363
  29.6 1.2 %copy.7 = f32[2,8]{1,0:T(2,128)} copy(f32[2,8]{1,0:T(2,128)} %shard_map.55) | data formatting | bytes 128
